TPU v7x, 512 devices: a whole 4x4x16 slice. The times are simulated.
512 devices in a mesh: dp: 4 (over y_hi, core), seq: 128 (over x, y_lo, z).
Axes of the slice: x: 4, y: 4 (y_hi: 2, y_lo: 2; y = y_hi * 2 + y_lo), z: 16, core: 2. Of those that a mesh axis runs over, the one named last changes fastest.
Arguments:
- clip_frames: bfloat16 [512, 16, 128, 128], P(('dp', 'seq')), parts along dimension 0, may hold values from -6 to 6
- cotangent: bfloat16 [512, 16, 128, 128], P(('dp', 'seq')), parts along dimension 0, may hold values from -6 to 6
- spatial_weight: bfloat16 [3, 3, 16, 16], replicated, may hold values from -0.5 to 0.5
- temporal_weight: bfloat16 [3, 3, 16, 16], replicated, may hold values from -0.4375 to 0.4375
Outputs:
- block_output: bfloat16 [512, 16, 128, 128], P(('dp', 'seq')), parts along dimension 0
- clip_grad: bfloat16 [512, 16, 128, 128], P(('dp', 'seq')), parts along dimension 0
- spatial_grad: float32 [12, 3, 16, 16], P('dp'), parts along dimension 0
- temporal_grad: float32 [12, 3, 16, 16], P('dp'), parts along dimension 0
There are 4 independent parts, one for each index of `dp`. A program takes and returns all parts, laid end to end along the dimension named above; an argument that names none is the same for every part. Nothing has to cross between parts.
All inputs are finite; a program needn't handle non-finite values.
Results may differ from a plain program's by a relative error of at most 0.0071.
Values may be sent and summed in bfloat16 or wider, within the bound.
A program may use at most 64 MiB of HBM per device.

v0:
```python
import math
import jax
import jax.numpy as jnp
from jax import lax
from jax.sharding import PartitionSpec as P


def shifted(values, row_step, col_step):
    row_count = values.shape[2]
    col_count = values.shape[3]
    padded = jnp.pad(values, ((0, 0), (0, 0), (1, 1), (1, 1)))
    return padded[
        :, :, 1 + row_step : 1 + row_step + row_count, 1 + col_step : 1 + col_step + col_count
    ]


def patches_of(values, orient):
    return jnp.concatenate(
        [shifted(values, orient * (a - 1), orient * (b - 1)) for a in range(3) for b in range(3)],
        axis=1,
    )


def time_shift(values, offset):
    length = values.shape[0]
    if offset > 0:
        return jnp.concatenate([values[offset:], jnp.zeros_like(values[:offset])], axis=0)
    if offset < 0:
        return jnp.concatenate([jnp.zeros_like(values[offset:]), values[:offset]], axis=0)
    return values


def silu_slope(preact):
    sigma = jax.nn.sigmoid(preact)
    return sigma * (1.0 + preact * (1.0 - sigma))


def temporal_forward(tiles, temporal_weight):
    states = [tiles]
    for layer in range(temporal_weight.shape[0]):
        dilation = 2**layer
        current = states[-1]
        branch = current.astype(jnp.float32)
        for tap in range(3):
            branch = branch + jnp.einsum(
                "tchw,cd->tdhw",
                time_shift(current, (tap - 1) * dilation),
                temporal_weight[layer, tap],
                preferred_element_type=jnp.float32,
            )
        states.append(branch.astype(jnp.bfloat16))
    return states


def body(clip_frames, cotangent, spatial_weight, temporal_weight):
    frames_dev, channels, row_count, col_count = clip_frames.shape
    layer_count = temporal_weight.shape[0]
    factor = 1.0 / math.sqrt(frames_dev * lax.axis_size("seq") * row_count * col_count)
    patches = patches_of(clip_frames, 1)
    flat_weight = spatial_weight.reshape(9 * channels, channels)
    preact = jnp.einsum("fkhw,kd->fdhw", patches, flat_weight, preferred_element_type=jnp.float32)
    activated = jax.nn.silu(preact).astype(jnp.bfloat16)
    tiles = lax.all_to_all(activated, "seq", split_axis=2, concat_axis=0, tiled=True)
    states = temporal_forward(tiles, temporal_weight)
    block_output = lax.all_to_all(states[-1], "seq", split_axis=0, concat_axis=2, tiled=True)
    grad_tiles = lax.all_to_all(cotangent, "seq", split_axis=2, concat_axis=0, tiled=True)
    gradient = grad_tiles
    layer_terms = [None] * layer_count
    for layer in reversed(range(layer_count)):
        dilation = 2**layer
        current = states[layer]
        local_term = jnp.stack(
            [
                jnp.einsum(
                    "tchw,tdhw->cd",
                    time_shift(current, (tap - 1) * dilation),
                    gradient,
                    preferred_element_type=jnp.float32,
                )
                for tap in range(3)
            ]
        )
        layer_terms[layer] = lax.psum(local_term, "seq")
        total = gradient.astype(jnp.float32)
        for tap in range(3):
            total = total + jnp.einsum(
                "tdhw,cd->tchw",
                time_shift(gradient, -(tap - 1) * dilation),
                temporal_weight[layer, tap],
                preferred_element_type=jnp.float32,
            )
        gradient = total.astype(jnp.bfloat16)
    grad_frames = lax.all_to_all(gradient, "seq", split_axis=0, concat_axis=2, tiled=True)
    slope = (grad_frames.astype(jnp.float32) * silu_slope(preact)).astype(jnp.bfloat16)
    spatial_term = jnp.einsum(
        "fkhw,fdhw->kd", patches, slope, preferred_element_type=jnp.float32
    ).reshape(3, 3, channels, channels)
    spatial_total = lax.psum(spatial_term, "seq")
    temporal_total = jnp.stack(layer_terms)
    mixing = spatial_weight.transpose(2, 0, 1, 3).reshape(channels, 9 * channels)
    clip_grad = jnp.einsum(
        "fkhw,ck->fchw", patches_of(slope, -1), mixing, preferred_element_type=jnp.float32
    ).astype(jnp.bfloat16)
    return (block_output, clip_grad, spatial_total * factor, temporal_total * factor)


def solution(mesh):
    placed = (P(("dp", "seq"), None, None, None), P(("dp", "seq"), None, None, None), P(), P())
    return jax.shard_map(
        body,
        mesh=mesh,
        in_specs=placed,
        out_specs=(
            P(("dp", "seq"), None, None, None),
            P(("dp", "seq"), None, None, None),
            P("dp", None, None, None),
            P("dp", None, None, None),
        ),
        check_vma=False,
    )
```

profile of v0, /device:TPU:16, one launch (start us, length us, event | category | flops | bytes accessed | tf_op | source)
XLA Modules:
  0.0 781.2 jit_solution(5370593056510770013)
XLA Ops:
  0.6 1.4 copy.73
  2.0 54.3 %all_to_all.57 = bf16[1,16,128,128]{3,1,0,2:T(8,128)(2,1)S(1)} all-to-all(bf16[1,16,128,128]{3,1,0,2:T(8,128)(2,1)S(1)} %copy.73), channel_id=1, replica_groups=mesh['dp'=4,'seq'=128] {'seq'}, dimensions={2} | all-to-all | bytes 1048576 | tf_op jit(solution)/shard_map/all_to_all | solution.py:66
  56.5 1.0 convolution_bitcast_fusion.6
  57.5 0.3 fusion.18
  57.8 0.3 fusion.28
  58.0 0.1 fusion.168
  58.2 0.3 convolution_bitcast_fusion.4
  58.4 0.3 convolution_bitcast_fusion.3
  58.7 0.3 fusion.30
  59.0 0.1 fusion.167
  59.2 0.3 convolution_bitcast_fusion.1
  59.4 0.3 convolution_bitcast_fusion
  59.7 1.1 fusion.35
  60.8 6.2 all-to-all-start.3
  67.1 0.3 copy.59
  67.4 1.0 fusion.40
  68.5 0.9 fusion.41
  69.4 1.0 fusion.42
  70.4 1.0 fusion.43
  71.4 1.2 constant_dynamic-update-slice_fusion
  72.6 1.0 fusion.44
  73.6 1.1 fusion.45
  74.7 0.9 fusion.46
  75.6 1.0 fusion.47
  76.7 23.6 %all-to-all-done.3 = bf16[128,16,1,128]{3,1,2,0:T(8,128)(2,1)S(1)} async-done(((bf16[128,16,1,128]{3,1,2,0:T(8,128)(2,1)}), bf16[128,16,1,128]{3,1,2,0:T(8,128)(2,1)S(1)}, u32[]{:S(2)}, u32[]{:S(2)}) %all-to-all-start.3) | async-done | bytes 524320 | tf_op jit(solution)/shard_map/all_to_all | solution.py:93
  100.3 3.9 fusion.39
  104.3 6.7 all-to-all-start
  111.1 3.7 fusion.56
  114.8 0.2 fusion.48
  115.1 0.3 fusion.50
  115.4 0.3 fusion.51
  115.7 0.3 fusion.52
  116.0 0.3 fusion.53
  116.4 0.3 fusion.55
  116.7 0.7 fusion.36
  117.4 0.9 copy.88
  118.4 25.7 %all-to-all-done = bf16[1,16,128,128]{3,1,0,2:T(8,128)(2,1)S(1)} async-done(((bf16[1,16,128,128]{3,1,0,2:T(8,128)(2,1)}), bf16[1,16,128,128]{3,1,0,2:T(8,128)(2,1)S(1)}, u32[]{:S(2)}, u32[]{:S(2)}) %all-to-all-start) | async-done | bytes 524320 | tf_op jit(solution)/shard_map/all_to_all | solution.py:63
  144.0 0.1 slice_bitcast_fusion.1
  144.2 0.3 convolution_bitcast_fusion.24
  144.5 0.3 convolution_bitcast_fusion.14
  144.8 0.3 convolution_bitcast_fusion.15
  145.2 0.4 fusion.33
  145.5 0.1 fusion.170
  145.7 0.3 convolution_bitcast_fusion.12
  146.0 0.3 convolution_bitcast_fusion.11
  146.4 0.4 fusion.32
  146.7 0.1 fusion.169
  146.9 0.3 convolution_bitcast_fusion.9
  147.2 0.4 copy-done.5
  147.7 0.3 convolution_bitcast_fusion.8
  148.0 1.2 fusion.34
  149.2 7.3 all-to-all-start.1
  156.5 0.3 convolution_bitcast_fusion.25
  156.8 1.4 convolution_bitcast_fusion.26
  158.2 1.4 convolution_bitcast_fusion.21
  159.6 1.4 convolution_bitcast_fusion.23
  160.9 0.3 convolution_bitcast_fusion.22
  161.3 0.3 convolution_bitcast_fusion.18
  161.6 0.3 convolution_bitcast_fusion.20
  161.9 0.3 convolution_bitcast_fusion.19
  162.3 615.6 %all-reduce.14 = (f32[3,3,16,16]{3,2,0,1:T(8,128)S(1)}, f32[1,3,16,16]{3,2,0,1:T(8,128)S(1)}, f32[1,3,16,16]{3,2,0,1:T(8,128)S(1)}, f32[1,3,16,16]{3,2,0,1:T(8,128)S(1)}) all-reduce(f32[3,3,16,16]{3,2,0,1:T(8,128)S(1)} %bitcast.469, f32[1,3,16,16]{3,2,0,1:T(8,128)S(1)} %maximum_bitcast_fusion.2, ...), channel_id=1, replica_groups=mesh['dp'=4,'seq'=128] {'seq'}, use_global_device_ids=true, to_apply=%region_0.1 | all-reduce | flops 4608 | bytes 36864 | tf_op jit(solution)/shard_map/psum | solution.py:98
  777.9 0.6 copy.89
  778.5 0.6 copy.90
  779.2 2.0 copy.87
  (31 shorter events, 0.6 us)
Async XLA Ops:
  0.6 56.8 %copy-start.8 = (bf16[3,3,16,16]{3,2,1,0:T(8,128)(2,1)S(1)}, bf16[3,3,16,16]{3,2,1,0:T(8,128)(2,1)}, u32[]{:S(2)}) copy-start(bf16[3,3,16,16]{3,2,1,0:T(8,128)(2,1)} %param.7) | copy-start | bytes 13828
  59.0 8.0 %copy-start.7 = (bf16[1,16,128,128]{3,2,1,0:T(8,128)(2,1)S(1)}, bf16[1,16,128,128]{3,2,1,0:T(8,128)(2,1)}, u32[]{:S(2)}) copy-start(bf16[1,16,128,128]{3,2,1,0:T(8,128)(2,1)} %param.4) | copy-start | bytes 1572868
  60.8 39.5 %all-to-all-start.3 = ((bf16[128,16,1,128]{3,1,2,0:T(8,128)(2,1)}), bf16[128,16,1,128]{3,1,2,0:T(8,128)(2,1)S(1)}, u32[]{:S(2)}, u32[]{:S(2)}) async-start(bf16[128,16,1,128]{3,1,2,0:T(8,128)(2,1)} %fusion.35), calls=%async_computation.3 | async-start | bytes 1048576 | tf_op jit(solution)/shard_map/all_to_all | solution.py:93
  67.4 32.9 %copy-start.9 = (bf16[3,3,16,16]{3,2,1,0:T(8,128)(2,1)S(1)}, bf16[3,3,16,16]{3,2,1,0:T(8,128)(2,1)}, u32[]{:S(2)}) copy-start(bf16[3,3,16,16]{3,2,1,0:T(8,128)(2,1)} %param.6) | copy-start | bytes 13828
  104.3 39.8 %all-to-all-start = ((bf16[1,16,128,128]{3,1,0,2:T(8,128)(2,1)}), bf16[1,16,128,128]{3,1,0,2:T(8,128)(2,1)S(1)}, u32[]{:S(2)}, u32[]{:S(2)}) async-start(bf16[1,16,128,128]{3,1,0,2:T(8,128)(2,1)} %get-tuple-element.21), calls=%async_computation | async-start | bytes 1048576 | tf_op jit(solution)/shard_map/all_to_all | solution.py:63
  144.2 1.5 copy-start
  145.7 1.5 copy-start.1
  145.7 1.5 copy-start.2
  146.9 0.8 copy-start.5
  146.9 1.1 copy-start.3
  149.2 630.0 %all-to-all-start.1 = ((bf16[128,16,1,128]{3,1,2,0:T(8,128)(2,1)}), bf16[128,16,1,128]{3,1,2,0:T(8,128)(2,1)}, u32[]{:S(2)}, u32[]{:S(2)}) async-start(bf16[128,16,1,128]{3,1,2,0:T(8,128)(2,1)} %fusion.34), calls=%async_computation.1 | async-start | bytes 1048576 | tf_op jit(solution)/shard_map/all_to_all | solution.py:65
  156.5 4.8 copy-start.6
  156.5 5.1 copy-start.4
where the time goes:
time: 782 us; the launch traced here: 781 us
  blocking collectives  670 us (86%)
  waiting for transfers between devices  49.3 us (6%)
  matrix products  22.2 us (3%)
  starting transfers between devices  20.2 us (3%)
  local copies, waits for them, and re-layouts  18.5 us (2%)
    psum x1, blocking collectives, body(): spatial_total = lax.psum(spatial_term, 'seq')  616 us
    all_to_all x1, blocking collectives, body(): lax.all_to_all(cotangent, 'seq', split_axis=2, concat_axis=0, tiled=True)  54.3 us
    all_to_all x1, waiting for transfers between devices, body(): lax.all_to_all(activated, 'seq', split_axis=2, concat_axis=0, tiled=True)  25.7 us
    all_to_all x1, waiting for transfers between devices, body(): lax.all_to_all(gradient, 'seq', split_axis=0, concat_axis=2, tiled=True)  23.6 us
    unnamed x42, local copies, waits for them, and re-layouts  16.2 us
  transfers between devices with their start and end apart: 3, of which 2 were waited for; matrix products, arithmetic and copies ran while one was open for 3% of the time, Pallas kernels for 0%

commit v1 on v0

--- a/solution.py
+++ b/solution.py
@@ -3,6 +3,12 @@
 import jax.numpy as jnp
 from jax import lax
 from jax.sharding import PartitionSpec as P
+
+
+def gather_and_add(value, axis):
+    parts = lax.all_gather(value, axis, axis=0, tiled=False)
+    total = parts.sum(axis=0)
+    return total
 
 
 def shifted(values, row_step, col_step):
@@ -95,7 +101,7 @@
     spatial_term = jnp.einsum(
         "fkhw,fdhw->kd", patches, slope, preferred_element_type=jnp.float32
     ).reshape(3, 3, channels, channels)
-    spatial_total = lax.psum(spatial_term, "seq")
+    spatial_total = gather_and_add(spatial_term, "seq")
     temporal_total = jnp.stack(layer_terms)
     mixing = spatial_weight.transpose(2, 0, 1, 3).reshape(channels, 9 * channels)
     clip_grad = jnp.einsum(

time: 782 us -> 804 us (1.028)
  between operations: 1.02 us -> 14.4 us
    unnamed x42 -> x38, local copies, waits for them, and re-layouts: 16.2 us -> 14.9 us
  transfers between devices with their start and end apart: 3 -> 4, of which waited for: 2 -> 2; matrix products, arithmetic and copies ran while one was open for 3% -> 4% of each run, Pallas kernels for 0% -> 0%
where the time goes in v1:
time: 804 us; the launch traced here: 803 us
  blocking collectives  673 us (84%)
  waiting for transfers between devices  48.8 us (6%)
  matrix products  23.2 us (3%)
  starting transfers between devices  20.2 us (3%)
  local copies, waits for them, and re-layouts  17.8 us (2%)
  between operations  14.4 us (2%)
    psum x1, blocking collectives, body(): layer_terms[layer] = lax.psum(local_term, 'seq')  619 us
    all_to_all x1, blocking collectives, body(): lax.all_to_all(cotangent, 'seq', split_axis=2, concat_axis=0, tiled=True)  54.3 us
    all_to_all x1, waiting for transfers between devices, body(): lax.all_to_all(activated, 'seq', split_axis=2, concat_axis=0, tiled=True)  25.1 us
    all_to_all x1, waiting for transfers between devices, body(): lax.all_to_all(gradient, 'seq', split_axis=0, concat_axis=2, tiled=True)  23.6 us
  transfers between devices with their start and end apart: 4, of which 2 were waited for; matrix products, arithmetic and copies ran while one was open for 4% of the time, Pallas kernels for 0%

profile of v1, /device:TPU:16, one launch (start us, length us, event | category | flops | bytes accessed | tf_op | source)
XLA Modules:
  0.0 803.3 jit_solution(6494352535721859480)
XLA Ops:
  7.2 1.4 copy.73
  8.6 54.3 %all_to_all.57 = bf16[1,16,128,128]{3,1,0,2:T(8,128)(2,1)S(1)} all-to-all(bf16[1,16,128,128]{3,1,0,2:T(8,128)(2,1)S(1)} %copy.73), channel_id=1, replica_groups=mesh['dp'=4,'seq'=128] {'seq'}, dimensions={2} | all-to-all | bytes 1048576 | tf_op jit(solution)/shard_map/all_to_all | solution.py:72
  63.0 1.0 convolution_bitcast_fusion.6
  64.0 0.3 fusion.20
  64.3 0.3 fusion.30
  64.6 0.1 fusion.172
  64.7 0.3 convolution_bitcast_fusion.4
  65.0 0.3 convolution_bitcast_fusion.3
  65.2 0.3 fusion.32
  65.6 0.1 fusion.171
  65.7 0.3 convolution_bitcast_fusion.1
  66.0 0.3 convolution_bitcast_fusion
  66.2 1.1 fusion.37
  67.3 6.2 all-to-all-start.3
  73.6 0.3 copy.59
  73.9 1.0 fusion.45
  75.0 1.0 fusion.46
  75.9 1.1 fusion.47
  77.0 1.0 fusion.48
  78.0 1.2 constant_dynamic-update-slice_fusion
  79.2 1.0 fusion.49
  80.2 1.0 fusion.50
  81.3 0.9 fusion.51
  82.2 1.0 fusion.52
  83.2 23.6 %all-to-all-done.3 = bf16[128,16,1,128]{3,1,2,0:T(8,128)(2,1)S(1)} async-done(((bf16[128,16,1,128]{3,1,2,0:T(8,128)(2,1)}), bf16[128,16,1,128]{3,1,2,0:T(8,128)(2,1)S(1)}, u32[]{:S(2)}, u32[]{:S(2)}) %all-to-all-start.3) | async-done | bytes 524320 | tf_op jit(solution)/shard_map/all_to_all | solution.py:99
  106.9 3.9 fusion.44
  110.8 6.5 all-to-all-start
  117.3 0.2 all-gather.3.cloned.1.call-start
  117.7 3.7 fusion.41
  121.3 0.6 copy.87
  122.0 0.2 fusion.53
  122.3 0.3 fusion.55
  122.6 0.3 fusion.56
  123.0 0.3 fusion.57
  123.3 0.3 fusion.58
  123.6 0.3 fusion.60
  123.9 0.7 fusion.38
  124.7 0.9 copy.89
  125.6 25.1 %all-to-all-done = bf16[1,16,128,128]{3,1,0,2:T(8,128)(2,1)S(1)} async-done(((bf16[1,16,128,128]{3,1,0,2:T(8,128)(2,1)}), bf16[1,16,128,128]{3,1,0,2:T(8,128)(2,1)S(1)}, u32[]{:S(2)}, u32[]{:S(2)}) %all-to-all-start) | async-done | bytes 524320 | tf_op jit(solution)/shard_map/all_to_all | solution.py:69
  150.8 0.3 convolution_bitcast_fusion.14
  151.2 0.3 convolution_bitcast_fusion.15
  151.5 0.4 fusion.35
  152.0 0.3 convolution_bitcast_fusion.12
  152.4 0.3 convolution_bitcast_fusion.11
  152.7 0.4 fusion.34
  153.2 0.3 convolution_bitcast_fusion.9
  153.5 0.4 copy-done.3
  154.0 0.3 convolution_bitcast_fusion.8
  154.3 1.2 fusion.36
  155.5 0.3 convolution_bitcast_fusion.26
  155.8 7.3 all-to-all-start.1
  163.1 0.3 convolution_bitcast_fusion.25
  163.4 1.4 convolution_bitcast_fusion.24
  164.8 1.4 convolution_bitcast_fusion.23
  166.2 1.4 convolution_bitcast_fusion.21
  167.5 1.4 convolution_bitcast_fusion.20
  168.9 0.3 convolution_bitcast_fusion.18
  169.2 0.3 convolution_bitcast_fusion.22
  169.6 0.3 convolution_bitcast_fusion.19
  169.9 618.9 %all-reduce.14 = (f32[1,3,16,16]{3,2,1,0:T(8,128)S(1)}, f32[1,3,16,16]{3,2,1,0:T(8,128)S(1)}, f32[1,3,16,16]{3,2,1,0:T(8,128)S(1)}) all-reduce(f32[1,3,16,16]{3,2,1,0:T(8,128)S(1)} %get-tuple-element.34, f32[1,3,16,16]{3,2,1,0:T(8,128)S(1)} %get-tuple-element.33, ...), channel_id=1, replica_groups=mesh['dp'=4,'seq'=128] {'seq'}, use_global_device_ids=true, to_apply=%region_3.4 | all-reduce | flops 2304 | bytes 18432 | tf_op jit(solution)/shard_map/psum | solution.py:89
  788.8 0.6 maximum_multiply_fusion
  789.5 4.4 reduce_sum.9
  793.9 0.6 broadcast_multiply_fusion
  794.5 2.0 copy.88
  (31 shorter events, 1.0 us)
Async XLA Ops:
  7.2 56.8 %copy-start.7 = (bf16[3,3,16,16]{3,2,1,0:T(8,128)(2,1)S(1)}, bf16[3,3,16,16]{3,2,1,0:T(8,128)(2,1)}, u32[]{:S(2)}) copy-start(bf16[3,3,16,16]{3,2,1,0:T(8,128)(2,1)} %param.7) | copy-start | bytes 13828
  65.6 8.0 copy-start.6
  67.3 39.5 %all-to-all-start.3 = ((bf16[128,16,1,128]{3,1,2,0:T(8,128)(2,1)}), bf16[128,16,1,128]{3,1,2,0:T(8,128)(2,1)S(1)}, u32[]{:S(2)}, u32[]{:S(2)}) async-start(bf16[128,16,1,128]{3,1,2,0:T(8,128)(2,1)} %fusion.37), calls=%async_computation.3 | async-start | bytes 1048576 | tf_op jit(solution)/shard_map/all_to_all | solution.py:99
  73.9 32.9 %copy-start.8 = (bf16[3,3,16,16]{3,2,1,0:T(8,128)(2,1)S(1)}, bf16[3,3,16,16]{3,2,1,0:T(8,128)(2,1)}, u32[]{:S(2)}) copy-start(bf16[3,3,16,16]{3,2,1,0:T(8,128)(2,1)} %param.6) | copy-start | bytes 13828
  110.8 39.9 %all-to-all-start = ((bf16[1,16,128,128]{3,1,0,2:T(8,128)(2,1)}), bf16[1,16,128,128]{3,1,0,2:T(8,128)(2,1)S(1)}, u32[]{:S(2)}, u32[]{:S(2)}) async-start(bf16[1,16,128,128]{3,1,0,2:T(8,128)(2,1)} %get-tuple-element.20), calls=%async_computation | async-start | bytes 1048576 | tf_op jit(solution)/shard_map/all_to_all | solution.py:69
  117.3 672.2 %all-gather.3.cloned.1.call-start = ((), (), s32[]{:S(2)}) async-start(), calls=%async_computation.4 | async-start | bytes 9510912 | tf_op jit(solution)/shard_map/all_gather | solution.py:9
  150.8 1.5 copy-start
  152.0 1.5 copy-start.1
  152.0 1.5 copy-start.2
  153.2 0.8 copy-start.3
  153.2 1.1 copy-start.5
  155.8 638.7 %all-to-all-start.1 = ((bf16[128,16,1,128]{3,1,2,0:T(8,128)(2,1)}), bf16[128,16,1,128]{3,1,2,0:T(8,128)(2,1)}, u32[]{:S(2)}, u32[]{:S(2)}) async-start(bf16[128,16,1,128]{3,1,2,0:T(8,128)(2,1)} %fusion.36), calls=%async_computation.1 | async-start | bytes 1048576 | tf_op jit(solution)/shard_map/all_to_all | solution.py:71
  163.1 5.8 copy-start.4
Sparse Core Ops, SparseCore 0:
  122.1 611.9 all-gather.2
